TPU v7x, 128 devices: a whole 4x4x4 slice. The times are simulated.
128 devices in a mesh: ctx: 16 (over y_lo, z, core), tp: 8 (over y_hi, x).
Axes of the slice: x: 4, y: 4 (y_hi: 2, y_lo: 2; y = y_hi * 2 + y_lo), z: 4, core: 2. Of those that a mesh axis runs over, the one named last changes fastest.
Arguments:
- tokens: bfloat16 [4096, 16384], P('tp', 'ctx'), may hold values from -6 to 6
- in_weight: bfloat16 [3, 4096, 4096], P(None, 'ctx', 'tp'), may hold values from -0.09375 to 0.09375
- short_taps: float32 [3, 4096, 3], P(None, 'tp'), may hold values from -3 to 3
- long_filter: float32 [4096, 16384], P('tp', 'ctx'), may hold values from -2 to 2
- skip_gain: float32 [4096], P('tp'), may hold values from -4 to 4
- out_weight: bfloat16 [4096, 4096], P('tp', 'ctx'), may hold values from -0.125 to 0.125
Outputs:
- layer_out: bfloat16 [4096, 16384], P('tp', 'ctx')
All inputs are finite; a program needn't handle non-finite values.
Results may differ from a plain program's by a relative error of at most 0.02.
Values may be sent and summed in bfloat16 or wider, within the bound.
A program may use at most 128 MiB of HBM per device.

v0:
```python
import math
import jax
import jax.numpy as jnp
from jax import lax
from jax.sharding import PartitionSpec as P

HIGHEST = lax.Precision.HIGHEST


def passed_along(shard, axis, by):
    count = lax.axis_size(axis)
    pairs = [(i, i + by) for i in range(count) if 0 <= i + by < count]
    return lax.ppermute(shard, axis, pairs)


def factor_length(full_len):
    inner_len = 1
    while inner_len * inner_len * 4 <= full_len and full_len % (inner_len * 2) == 0:
        inner_len = inner_len * 2
    return (inner_len, full_len // inner_len)


def phase_table(rows_count, cols_count, period):
    row_ids = jnp.arange(rows_count, dtype=jnp.int32)[:, None]
    col_ids = jnp.arange(cols_count, dtype=jnp.int32)[None, :]
    angles = (row_ids * col_ids % period).astype(jnp.float32) * (2.0 * math.pi / period)
    return (jnp.cos(angles), jnp.sin(angles))


def make_tables(full_len):
    inner_len, outer_len = factor_length(full_len)
    cos_inner, sin_inner = phase_table(inner_len, inner_len, inner_len)
    cos_outer, sin_outer = phase_table(outer_len // 2, outer_len, outer_len)
    cos_twist, sin_twist = phase_table(outer_len, inner_len, full_len)
    return (cos_inner, sin_inner, cos_outer, sin_outer, cos_twist, sin_twist)


def spectrum(signal, tables):
    cos_inner, sin_inner, cos_outer, sin_outer, cos_twist, sin_twist = tables
    channels = signal.shape[0]
    grid_view = signal.reshape(channels, cos_outer.shape[0], cos_inner.shape[0])
    part_re = jnp.einsum("cmn,mk->ckn", grid_view, cos_outer, precision=HIGHEST)
    part_im = -jnp.einsum("cmn,mk->ckn", grid_view, sin_outer, precision=HIGHEST)
    twist_re = part_re * cos_twist + part_im * sin_twist
    twist_im = part_im * cos_twist - part_re * sin_twist
    freq_re = jnp.einsum("ckn,nj->ckj", twist_re, cos_inner, precision=HIGHEST) + jnp.einsum(
        "ckn,nj->ckj", twist_im, sin_inner, precision=HIGHEST
    )
    freq_im = jnp.einsum("ckn,nj->ckj", twist_im, cos_inner, precision=HIGHEST) - jnp.einsum(
        "ckn,nj->ckj", twist_re, sin_inner, precision=HIGHEST
    )
    return (freq_re, freq_im)


def spectrum_back(freq_re, freq_im, tables):
    cos_inner, sin_inner, cos_outer, sin_outer, cos_twist, sin_twist = tables
    mix_re = jnp.einsum("ckj,jn->ckn", freq_re, cos_inner, precision=HIGHEST) - jnp.einsum(
        "ckj,jn->ckn", freq_im, sin_inner, precision=HIGHEST
    )
    mix_im = jnp.einsum("ckj,jn->ckn", freq_im, cos_inner, precision=HIGHEST) + jnp.einsum(
        "ckj,jn->ckn", freq_re, sin_inner, precision=HIGHEST
    )
    turn_re = mix_re * cos_twist - mix_im * sin_twist
    turn_im = mix_im * cos_twist + mix_re * sin_twist
    channels = freq_re.shape[0]
    length = cos_outer.shape[0] * cos_inner.shape[0]
    norm_factor = 1.0 / (cos_outer.shape[1] * cos_inner.shape[0])
    real_out = jnp.einsum("ckn,mk->cmn", turn_re, cos_outer, precision=HIGHEST) - jnp.einsum(
        "ckn,mk->cmn", turn_im, sin_outer, precision=HIGHEST
    )
    real_out = real_out.reshape(channels, length) * norm_factor
    return real_out


def per_device(tokens, in_weight, short_taps, long_filter, skip_gain, out_weight):
    steps_dev = tokens.shape[1]
    filter_groups = lax.all_to_all(
        long_filter.astype(jnp.bfloat16), "ctx", split_axis=0, concat_axis=1, tiled=True
    ).astype(long_filter.dtype)
    features_all = lax.all_gather(tokens, "tp", axis=0, tiled=True)
    sources = (features_all,)
    shard_rows = lax.all_gather(in_weight, "ctx", axis=1, tiled=True)
    results = tuple(
        (
            jnp.einsum("sic,it->sct", shard_rows, source, preferred_element_type=jnp.float32)
            for source in sources
        )
    )
    projected = results[0]
    before = passed_along(projected[:, :, steps_dev - 2 :], "ctx", 1)
    prev_one = jnp.concatenate([before[:, :, 1:], projected[:, :, :-1]], axis=2)
    prev_two = jnp.concatenate([before, projected[:, :, :-2]], axis=2)
    mixed_short = (
        short_taps[:, :, 0:1] * projected
        + short_taps[:, :, 1:2] * prev_one
        + short_taps[:, :, 2:3] * prev_two
    )
    gated_rows = (mixed_short[1] * mixed_short[2]).astype(jnp.bfloat16)
    signal = lax.all_to_all(gated_rows, "ctx", split_axis=0, concat_axis=1, tiled=True)
    tables = make_tables(2 * signal.shape[1])
    sig_re, sig_im = spectrum(signal.astype(jnp.float32), tables)
    fil_re, fil_im = spectrum(filter_groups, tables)
    prod_re = sig_re * fil_re - sig_im * fil_im
    prod_im = sig_re * fil_im + sig_im * fil_re
    long_rows = spectrum_back(prod_re, prod_im, tables)
    long_rows = long_rows.astype(jnp.bfloat16)
    returned = lax.all_to_all(long_rows, "ctx", split_axis=1, concat_axis=0, tiled=True)
    hidden = (
        (returned.astype(jnp.float32) + skip_gain[:, None] * gated_rows.astype(jnp.float32))
        * mixed_short[0]
    ).astype(jnp.bfloat16)
    whole_out = lax.all_gather(out_weight, "ctx", axis=1, tiled=True)
    return lax.psum_scatter(
        jnp.einsum("cd,ct->dt", whole_out, hidden, preferred_element_type=jnp.float32).astype(
            jnp.bfloat16
        ),
        "tp",
        scatter_dimension=0,
        tiled=True,
    )


def solution(mesh):
    placed = (
        P("tp", "ctx"),
        P(None, "ctx", "tp"),
        P(None, "tp", None),
        P("tp", "ctx"),
        P("tp"),
        P("tp", "ctx"),
    )
    return jax.shard_map(
        per_device, mesh=mesh, in_specs=placed, out_specs=P("tp", "ctx"), check_vma=False
    )
```

profile of v0, /device:TPU:1, one launch (start us, length us, event | category | flops | bytes accessed | tf_op | source)
XLA Modules:
  0.0 480.2 jit_solution(12676117775673328608)
XLA Ops:
  6.5 0.0 all-gather.6.cloned.1.call-start
  6.5 0.7 all-gather.6.cloned.1.call-update
  7.3 0.0 copy-start.13
  7.3 0.0 all-gather.4.cloned.1.call-start
  7.3 2.3 copy.25
  9.6 0.0 all-gather.4.cloned.1.call-update
  9.7 0.0 copy-done.12
  9.7 1.1 convert_element_type.122
  10.8 7.8 %all-to-all-start.1 = ((bf16[16,32,1024]{2,1,0:T(8,128)(2,1)}), bf16[16,32,1024]{2,1,0:T(8,128)(2,1)S(1)}, u32[]{:S(2)}, u32[]{:S(2)}) async-start(bf16[16,32,1024]{2,1,0:T(8,128)(2,1)} %bitcast.11), calls=%async_computation.1 | async-start | bytes 2097152 | tf_op jit(solution)/shard_map/all_to_all | solution.py:77
  18.6 0.0 all-gather.8.cloned.1.call-start
  18.7 0.7 all-gather.8.cloned.1.call-update
  19.4 0.0 copy-done.13
  19.4 0.5 fusion.94
  20.0 19.7 %all-to-all-done.1 = bf16[16,32,1024]{2,1,0:T(8,128)(2,1)S(1)} async-done(((bf16[16,32,1024]{2,1,0:T(8,128)(2,1)}), bf16[16,32,1024]{2,1,0:T(8,128)(2,1)S(1)}, u32[]{:S(2)}, u32[]{:S(2)}) %all-to-all-start.1) | async-done | bytes 1048608 | tf_op jit(solution)/shard_map/all_to_all | solution.py:77
  39.6 0.6 copy.32
  40.2 0.5 reshape.70
  40.7 2.3 fusion.64
  43.1 0.0 copy-start
  43.1 2.3 fusion.60
  45.4 2.0 copy-done.2
  47.4 5.6 %fusion.6 = f32[32,256,128]{2,1,0:T(8,128)} fusion(f32[256,32,128]{2,0,1:T(8,128)S(1)} %fusion.64, f32[256,32,128]{2,0,1:T(8,128)S(1)} %fusion.60, f32[256,128]{1,0:T(8,128)S(1)} %get-tuple-element.12, f32[256,128]{1,0:T(8,128)S(1)} %get-tuple-element.13), kind=kOutput, calls=%fused_computation.9 | convolution fusion | flops 1615036416 | bytes 12845056 | tf_op jit(solution)/shard_map/ckn,nj->ckj/dot_general | solution.py:46
  53.0 74.5 %all-gather.6.cloned.1.call-done = bf16[4096,1024]{1,0:T(8,128)(2,1)} async-done(((bf16[512,1024]{1,0:T(8,128)(2,1)}), bf16[4096,1024]{1,0:T(8,128)(2,1)}) %all-gather.6.cloned.1.call-update) | async-done | bytes 8388624 | tf_op jit(solution)/shard_map/all_gather | solution.py:80
  127.5 79.9 %all-gather.4.cloned.1.call-done = bf16[3,4096,512]{1,2,0:T(8,128)(2,1)} async-done(((bf16[3,256,512]{1,2,0:T(8,128)(2,1)}), bf16[3,4096,512]{1,2,0:T(8,128)(2,1)}) %all-gather.4.cloned.1.call-update) | async-done | bytes 12582928 | tf_op jit(solution)/shard_map/all_gather | solution.py:82
  207.3 16.7 %fusion = f32[3,512,1024]{2,1,0:T(8,128)S(1)} fusion(bf16[3,4096,512]{1,2,0:T(8,128)(2,1)} %all-gather.4.cloned.1.call-done, bf16[4096,1024]{1,0:T(8,128)(2,1)} %all-gather.6.cloned.1.call-done), kind=kOutput, calls=%fused_computation | convolution fusion | flops 12884901888 | bytes 27262976 | tf_op jit(solution)/shard_map/sic,it->sct/dot_general | solution.py:85
  224.1 2.6 copy-done.4
  226.7 0.3 slice.40
  227.0 0.3 copy.26
  227.2 2.8 collective-permute-start
  230.0 8.5 %fusion.34 = f32[32,256,128]{2,1,0:T(8,128)} fusion(f32[32,256,128]{2,1,0:T(8,128)} %fusion.6, f32[256,32,128]{2,0,1:T(8,128)} %copy-done, f32[256,32,128]{2,0,1:T(8,128)} %copy-done.2, f32[256,128]{1,0:T(8,128)S(1)} %get-tuple-element.12, f32[256,128]{1,0:T(8,128)S(1)} %get-tuple-element.13), kind=kOutput, calls=%fused_computation.39 | convolution fusion | flops 1616084992 | bytes 17039360 | tf_op jit(solution)/shard_map/ckn,nj->ckj/dot_general | solution.py:46
  238.5 0.0 collective-permute-done
  238.5 0.3 copy.27
  238.8 0.3 copy.28
  239.1 9.3 %fusion.3 = f32[3,512,1024]{2,1,0:T(8,128)S(1)} fusion(f32[3,512,1023]{2,1,0:T(8,128)} %bitcast.120, f32[3,512,1]{2,1,0:T(8,128)S(1)} %copy.27, f32[3,512,1022]{2,1,0:T(8,128)} %bitcast.121, f32[3,512,2]{2,1,0:T(8,128)S(1)} %copy.28, f32[3,512,1024]{2,1,0:T(8,128)} %copy-done.4, f32[3,512]{1,0:T(4,128)S(1)} %get-tuple-element.10, ...), kind=kLoop, calls=%fused_computation.5 | loop fusion | flops 11010048 | bytes 25184256 | tf_op jit(solution)/shard_map/add | solution.py:94
  248.4 2.6 copy-done.5
  251.0 1.3 fusion.42
  252.3 4.5 all-to-all-start
  256.9 0.0 reduce-scatter.2.cloned.1.call-start
  256.9 6.8 %fusion.4 = f32[32,256,128]{2,1,0:T(8,128)S(1)} fusion(f32[256,32,128]{2,0,1:T(8,128)} %copy-done, f32[256,32,128]{2,0,1:T(8,128)} %copy-done.2, f32[256,128]{1,0:T(8,128)S(1)} %get-tuple-element.12, f32[256,128]{1,0:T(8,128)S(1)} %get-tuple-element.13), kind=kOutput, calls=%fused_computation.7 | convolution fusion | flops 1615036416 | bytes 12845056 | tf_op jit(solution)/shard_map/ckn,nj->ckj/dot_general | solution.py:49
  263.7 5.7 %fusion.37 = f32[32,256,128]{2,1,0:T(8,128)} fusion(f32[32,256,128]{2,1,0:T(8,128)S(1)} %fusion.4, f32[256,32,128]{2,0,1:T(8,128)S(1)} %copy-done.1, f32[256,32,128]{2,0,1:T(8,128)S(1)} %copy-done.3, f32[256,128]{1,0:T(8,128)S(1)} %get-tuple-element.12, f32[256,128]{1,0:T(8,128)S(1)} %get-tuple-element.13), kind=kOutput, calls=%fused_computation.40 | convolution fusion | flops 1616084992 | bytes 17039360 | tf_op jit(solution)/shard_map/ckn,nj->ckj/dot_general | solution.py:49
  269.4 3.2 all-to-all-done
  272.7 0.6 copy.29
  273.3 1.0 reshape.69
  274.2 2.3 fusion.66
  276.5 2.3 fusion.62
  278.8 4.3 fusion.14
  283.2 5.5 %fusion.12 = f32[32,256,128]{2,1,0:T(8,128)S(1)} fusion(f32[256,32,128]{2,0,1:T(8,128)S(1)} %fusion.66, f32[256,32,128]{2,0,1:T(8,128)S(1)} %fusion.62, f32[256,128]{1,0:T(8,128)} %copy-done.6, f32[256,128]{1,0:T(8,128)} %copy-done.9), kind=kOutput, calls=%fused_computation.15 | convolution fusion | flops 1615036416 | bytes 12845056 | tf_op jit(solution)/shard_map/ckn,nj->ckj/dot_general | solution.py:49
  288.7 5.7 %fusion.28 = f32[32,256,128]{2,1,0:T(8,128)} fusion(f32[32,256,128]{2,1,0:T(8,128)S(1)} %fusion.14, f32[256,32,128]{2,0,1:T(8,128)S(1)} %fusion.66, f32[256,32,128]{2,0,1:T(8,128)S(1)} %fusion.62, f32[256,128]{1,0:T(8,128)S(1)} %copy-done.7, f32[256,128]{1,0:T(8,128)S(1)} %copy-done.10), kind=kOutput, calls=%fused_computation.37 | convolution fusion | flops 1616084992 | bytes 17039360 | tf_op jit(solution)/shard_map/ckn,nj->ckj/dot_general | solution.py:46
  294.4 8.4 %multiply_add_fusion = (f32[32,256,128]{2,1,0:T(8,128)S(1)}, f32[32,256,128]{2,1,0:T(8,128)S(1)}) fusion(f32[32,256,128]{2,1,0:T(8,128)} %fusion.34, f32[32,256,128]{2,1,0:T(8,128)} %fusion.28, f32[32,256,128]{2,1,0:T(8,128)} %fusion.37, f32[32,256,128]{2,1,0:T(8,128)S(1)} %fusion.12, f32[256,128]{1,0:T(8,128)} %copy-done.6, ...), kind=kOutput, calls=%fused_computation.31 | convolution fusion | flops 1622376448 | bytes 33816576 | tf_op jit(solution)/shard_map/ckn,nj->ckj/dot_general | solution.py:49
  302.8 3.7 fusion.86
  306.5 3.7 fusion.84
  310.1 3.7 convolution_subtract_fusion
  313.8 3.9 convolution_add_fusion
  317.7 3.3 fusion.20
  321.0 3.4 fusion.50
  324.4 0.0 copy-start.14
  324.4 0.5 convert_element_type.125
  324.9 0.6 copy.35
  325.5 19.1 %all_to_all.39 = bf16[32,16,1024]{2,0,1:T(8,128)(2,1)S(1)} all-to-all(bf16[32,16,1024]{2,0,1:T(8,128)(2,1)S(1)} %copy.35), channel_id=1, replica_groups=mesh['ctx'=16,'tp'=8] {'ctx'}, dimensions={1} | all-to-all | bytes 2097152 | tf_op jit(solution)/shard_map/all_to_all | solution.py:107
  344.6 3.4 fusion.41
  348.0 0.0 all-gather.8.cloned.1.call-done
  348.0 9.0 %convert_bitcast_fusion = bf16[4096,1024]{0,1:T(8,128)(2,1)} fusion(bf16[512,1024]{1,0:T(8,128)(2,1)S(1)} %fusion.41, bf16[512,4096]{1,0:T(8,128)(2,1)} %all-gather.8.cloned.1.call-done), kind=kOutput, calls=%fused_computation.2 | convolution fusion | flops 4299161600 | bytes 13631488 | tf_op jit(solution)/shard_map/cd,ct->dt/dot_general | solution.py:114
  357.0 0.0 reduce-scatter.2.cloned.1.call-update
  357.0 113.9 %reduce-scatter.2.cloned.1.call-done = bf16[512,1024]{0,1:T(8,128)(2,1)} async-done(((bf16[4096,1024]{0,1:T(8,128)(2,1)}), bf16[512,1024]{0,1:T(8,128)(2,1)}) %reduce-scatter.2.cloned.1.call-update) | async-done | bytes 1048592 | tf_op jit(solution)/shard_map/reduce_scatter | solution.py:113
  471.0 2.3 copy.36
  (26 shorter events, 0.1 us)
Async XLA Ops:
  6.5 3.1 copy-start.12
  6.5 120.9 %all-gather.6.cloned.1.call-start = ((), (), s32[]{:S(2)}) async-start(), calls=%async_computation.5 | async-start | bytes 9437184 | tf_op jit(solution)/shard_map/all_gather | solution.py:80
  7.3 12.1 %copy-start.13 = (f32[3,512,3]{1,2,0:T(4,128)S(1)}, f32[3,512,3]{1,2,0:T(4,128)}, u32[]{:S(2)}) copy-start(f32[3,512,3]{1,2,0:T(4,128)} %param.8) | copy-start | bytes 55300
  7.3 200.1 %all-gather.4.cloned.1.call-start = ((), (), s32[]{:S(2)}) async-start(), calls=%async_computation.4 | async-start | bytes 13369344 | tf_op jit(solution)/shard_map/all_gather | solution.py:82
  10.8 28.8 %all-to-all-start.1 = ((bf16[16,32,1024]{2,1,0:T(8,128)(2,1)}), bf16[16,32,1024]{2,1,0:T(8,128)(2,1)S(1)}, u32[]{:S(2)}, u32[]{:S(2)}) async-start(bf16[16,32,1024]{2,1,0:T(8,128)(2,1)} %bitcast.11), calls=%async_computation.1 | async-start | bytes 2097152 | tf_op jit(solution)/shard_map/all_to_all | solution.py:77
  18.6 329.4 %all-gather.8.cloned.1.call-start = ((), (), s32[]{:S(2)}) async-start(), calls=%async_computation.6 | async-start | bytes 4456448 | tf_op jit(solution)/shard_map/all_gather | solution.py:112
  20.0 258.9 %copy-start.6 = (f32[256,128]{1,0:T(8,128)}, f32[256,128]{1,0:T(8,128)S(1)}, u32[]{:S(2)}) copy-start(f32[256,128]{1,0:T(8,128)S(1)} %get-tuple-element.12) | copy-start | bytes 393220
  20.0 258.9 %copy-start.9 = (f32[256,128]{1,0:T(8,128)}, f32[256,128]{1,0:T(8,128)S(1)}, u32[]{:S(2)}) copy-start(f32[256,128]{1,0:T(8,128)S(1)} %get-tuple-element.13) | copy-start | bytes 393220
  43.1 2.4 copy-start
  45.4 2.0 copy-start.2
  224.1 2.6 copy-start.4
  227.2 11.3 %collective-permute-start = (f32[3,512,2]{1,2,0:T(2,128)S(1)}, f32[3,512,2]{1,2,0:T(2,128)S(1)}, u32[]{:S(2)}, u32[]{:S(2)}) collective-permute-start(f32[3,512,2]{1,2,0:T(2,128)S(1)} %copy.26), channel_id=1, source_target_pairs={{0,8},{8,16},{16,24},{24,32},{32,40},{40,48},{48,56},{56,64},{64,7... | collective-permute-start | bytes 36872 | tf_op jit(solution)/shard_map/ppermute | solution.py:13
  248.4 2.6 copy-start.5
  252.3 20.3 %all-to-all-start = ((bf16[16,32,1024]{2,1,0:T(8,128)(2,1)}), bf16[16,32,1024]{2,1,0:T(8,128)(2,1)S(1)}, u32[]{:S(2)}, u32[]{:S(2)}) async-start(bf16[16,32,1024]{2,1,0:T(8,128)(2,1)} %bitcast.3), calls=%async_computation | async-start | bytes 2097152 | tf_op jit(solution)/shard_map/all_to_all | solution.py:99
  256.9 214.1 %reduce-scatter.2.cloned.1.call-start = ((), (), s32[]{:S(2)}) async-start(), calls=%async_computation.7 | async-start | bytes 9437184 | tf_op jit(solution)/shard_map/reduce_scatter | solution.py:113
  256.9 6.8 %copy-start.1 = (f32[256,32,128]{2,0,1:T(8,128)S(1)}, f32[256,32,128]{2,0,1:T(8,128)}, u32[]{:S(2)}) copy-start(f32[256,32,128]{2,0,1:T(8,128)} %copy-done) | copy-start | bytes 12582916
  256.9 6.8 %copy-start.3 = (f32[256,32,128]{2,0,1:T(8,128)S(1)}, f32[256,32,128]{2,0,1:T(8,128)}, u32[]{:S(2)}) copy-start(f32[256,32,128]{2,0,1:T(8,128)} %copy-done.2) | copy-start | bytes 12582916
  283.2 5.5 %copy-start.7 = (f32[256,128]{1,0:T(8,128)S(1)}, f32[256,128]{1,0:T(8,128)}, u32[]{:S(2)}) copy-start(f32[256,128]{1,0:T(8,128)} %copy-done.6) | copy-start | bytes 393220
  283.2 5.5 %copy-start.10 = (f32[256,128]{1,0:T(8,128)S(1)}, f32[256,128]{1,0:T(8,128)}, u32[]{:S(2)}) copy-start(f32[256,128]{1,0:T(8,128)} %copy-done.9) | copy-start | bytes 393220
  313.8 3.9 copy-start.8
  313.8 3.9 copy-start.11
  324.4 20.2 %copy-start.14 = (f32[512]{0:T(512)S(1)}, f32[512]{0:T(512)}, u32[]{:S(2)}) copy-start(f32[512]{0:T(512)} %param.10) | copy-start | bytes 6148
Sparse Core Ops, SparseCore 0:
  9.7 117.7 all-gather.5
  129.1 78.2 all-gather.3
  209.0 45.4 all-gather.7
  357.2 113.7 reduce-scatter.1
where the time goes:
time: 489 us; the launch traced here: 480 us
  waiting for transfers between devices  293 us (60%)
  matrix products  107 us (22%)
  blocking collectives  19.1 us (4%)
  local copies, waits for them, and re-layouts  16.7 us (3%)
  other arithmetic  15.6 us (3%)
  starting transfers between devices  15.3 us (3%)
  between operations  14 us (3%)
    reduce_scatter x1, waiting for transfers between devices, per_device(): lax.psum_scatter(jnp.einsum('cd,ct->dt', whole_out, hidden, preferred_ele...  114 us
    all_gather x1, waiting for transfers between devices, per_device(): shard_rows = lax.all_gather(in_weight, 'ctx', axis=1, tiled=True)  79.9 us
    all_gather x1, waiting for transfers between devices, per_device(): features_all = lax.all_gather(tokens, 'tp', axis=0, tiled=True)  74.5 us
    all_to_all x1, waiting for transfers between devices, per_device(): lax.all_to_all(long_filter.astype(jnp.bfloat16), 'ctx', split_axis=0, con...  19.7 us
    all_to_all x1, blocking collectives, per_device(): lax.all_to_all(long_rows, 'ctx', split_axis=1, concat_axis=0, tiled=True)  19.1 us
    dot_general x1, matrix products, per_device(): jnp.einsum('sic,it->sct', shard_rows, source, preferred_element_type=jnp....  16.7 us
    dot_general x2, matrix products, spectrum(): jnp.einsum('ckn,nj->ckj', twist_re, sin_inner, precision=HIGHEST)  14.1 us
    dot_general x2, matrix products, spectrum(): jnp.einsum('ckn,nj->ckj', twist_re, cos_inner, precision=HIGHEST)  14.1 us
  transfers between devices with their start and end apart: 7, of which 5 were waited for; matrix products, arithmetic and copies ran while one was open for 25% of the time, Pallas kernels for 0%

commit v1 on v0

--- a/solution.py
+++ b/solution.py
@@ -5,6 +5,15 @@
 from jax.sharding import PartitionSpec as P
 
 HIGHEST = lax.Precision.HIGHEST
+wait_digits_in = lambda piece_in, mesh_ax: jnp.concatenate(
+    lax.all_to_all(
+        jnp.stack(jnp.split(piece_in, lax.axis_size(mesh_ax), axis=1)),
+        mesh_ax,
+        split_axis=0,
+        concat_axis=0,
+    ),
+    axis=0,
+)
 
 
 def passed_along(shard, axis, by):
@@ -104,7 +113,7 @@
     prod_im = sig_re * fil_im + sig_im * fil_re
     long_rows = spectrum_back(prod_re, prod_im, tables)
     long_rows = long_rows.astype(jnp.bfloat16)
-    returned = lax.all_to_all(long_rows, "ctx", split_axis=1, concat_axis=0, tiled=True)
+    returned = wait_digits_in(long_rows, "ctx")
     hidden = (
         (returned.astype(jnp.float32) + skip_gain[:, None] * gated_rows.astype(jnp.float32))
         * mixed_short[0]

time: 489 us -> 500 us (1.022)
  blocking collectives: 19.1 us -> 0 us
  waiting for transfers between devices: 293 us -> 308 us
  local copies, waits for them, and re-layouts: 16.7 us -> 26.3 us
    all_to_all x1 -> x0, blocking collectives: 19.1 us -> none  [per_device(): lax.all_to_all(long_rows, 'ctx', split_axis=1, concat_axis=0, tiled=True)]
    all_to_all x0 -> x1, waiting for transfers between devices: none -> 15.6 us  [lax.all_to_all(jnp.stack(jnp.split(piece_in, lax.axis_size(mesh_ax), axis...]
    unnamed x33 -> x49, local copies, waits for them, and re-layouts: 9.58 us -> 19.7 us
  transfers between devices with their start and end apart: 7 -> 8, of which waited for: 5 -> 6; matrix products, arithmetic and copies ran while one was open for 25% -> 26% of each run, Pallas kernels for 0% -> 0%
where the time goes in v1:
time: 500 us; the launch traced here: 491 us
  waiting for transfers between devices  308 us (62%)
  matrix products  110 us (22%)
  local copies, waits for them, and re-layouts  26.3 us (5%)
  starting transfers between devices  19.8 us (4%)
  between operations  14 us (3%)
  other arithmetic  12.2 us (2%)
    reduce_scatter x1, waiting for transfers between devices, per_device(): lax.psum_scatter(jnp.einsum('cd,ct->dt', whole_out, hidden, preferred_ele...  114 us
    all_gather x1, waiting for transfers between devices, per_device(): shard_rows = lax.all_gather(in_weight, 'ctx', axis=1, tiled=True)  79.9 us
    all_gather x1, waiting for transfers between devices, per_device(): features_all = lax.all_gather(tokens, 'tp', axis=0, tiled=True)  74.4 us
    unnamed x49, local copies, waits for them, and re-layouts  19.7 us
    all_to_all x1, waiting for transfers between devices, per_device(): lax.all_to_all(long_filter.astype(jnp.bfloat16), 'ctx', split_axis=0, con...  19.7 us
    dot_general x2, matrix products, spectrum(): jnp.einsum('ckn,nj->ckj', twist_re, sin_inner, precision=HIGHEST)  16.9 us
    dot_general x1, matrix products, per_device(): jnp.einsum('sic,it->sct', shard_rows, source, preferred_element_type=jnp....  16.7 us
    all_to_all x1, waiting for transfers between devices, lax.all_to_all(jnp.stack(jnp.split(piece_in, lax.axis_size(mesh_ax), axis...  15.6 us
  transfers between devices with their start and end apart: 8, of which 6 were waited for; matrix products, arithmetic and copies ran while one was open for 26% of the time, Pallas kernels for 0%

profile of v1, /device:TPU:1, one launch (start us, length us, event | category | flops | bytes accessed | tf_op | source)
XLA Modules:
  0.0 490.6 jit_solution(2270216014508966554)
XLA Ops:
  6.5 0.7 all-gather.6.cloned.1.call-update
  7.3 2.3 copy.23
  9.7 1.1 convert_element_type.118
  10.8 7.8 %all-to-all-start.1 = ((bf16[16,32,1024]{2,1,0:T(8,128)(2,1)}), bf16[16,32,1024]{2,1,0:T(8,128)(2,1)S(1)}, u32[]{:S(2)}, u32[]{:S(2)}) async-start(bf16[16,32,1024]{2,1,0:T(8,128)(2,1)} %bitcast.11), calls=%async_computation.1 | async-start | bytes 2097152 | tf_op jit(solution)/shard_map/all_to_all | solution.py:86
  18.7 0.7 all-gather.8.cloned.1.call-update
  19.4 0.5 fusion.110
  20.0 19.7 %all-to-all-done.1 = bf16[16,32,1024]{2,1,0:T(8,128)(2,1)S(1)} async-done(((bf16[16,32,1024]{2,1,0:T(8,128)(2,1)}), bf16[16,32,1024]{2,1,0:T(8,128)(2,1)S(1)}, u32[]{:S(2)}, u32[]{:S(2)}) %all-to-all-start.1) | async-done | bytes 1048608 | tf_op jit(solution)/shard_map/all_to_all | solution.py:86
  39.7 0.6 copy.30
  40.2 0.5 reshape.67
  40.7 2.3 fusion.60
  43.1 2.3 fusion.64
  45.5 2.0 copy-done.2
  47.5 5.6 %fusion.4 = f32[32,256,128]{2,1,0:T(8,128)} fusion(f32[256,32,128]{2,0,1:T(8,128)S(1)} %fusion.64, f32[256,32,128]{2,0,1:T(8,128)S(1)} %fusion.60, f32[256,128]{1,0:T(8,128)S(1)} %get-tuple-element.12, f32[256,128]{1,0:T(8,128)S(1)} %get-tuple-element.13), kind=kOutput, calls=%fused_computation.7 | convolution fusion | flops 1615036416 | bytes 12845056 | tf_op jit(solution)/shard_map/ckn,nj->ckj/dot_general | solution.py:58
  53.1 74.4 %all-gather.6.cloned.1.call-done = bf16[4096,1024]{1,0:T(8,128)(2,1)} async-done(((bf16[512,1024]{1,0:T(8,128)(2,1)}), bf16[4096,1024]{1,0:T(8,128)(2,1)}) %all-gather.6.cloned.1.call-update) | async-done | bytes 8388624 | tf_op jit(solution)/shard_map/all_gather | solution.py:89
  127.5 79.9 %all-gather.4.cloned.1.call-done = bf16[3,4096,512]{1,2,0:T(8,128)(2,1)} async-done(((bf16[3,256,512]{1,2,0:T(8,128)(2,1)}), bf16[3,4096,512]{1,2,0:T(8,128)(2,1)}) %all-gather.4.cloned.1.call-update) | async-done | bytes 12582928 | tf_op jit(solution)/shard_map/all_gather | solution.py:91
  207.3 16.7 %fusion = f32[3,512,1024]{2,1,0:T(8,128)S(1)} fusion(bf16[3,4096,512]{1,2,0:T(8,128)(2,1)} %all-gather.4.cloned.1.call-done, bf16[4096,1024]{1,0:T(8,128)(2,1)} %all-gather.6.cloned.1.call-done), kind=kOutput, calls=%fused_computation | convolution fusion | flops 12884901888 | bytes 27262976 | tf_op jit(solution)/shard_map/sic,it->sct/dot_general | solution.py:94
  224.1 2.6 copy-done.4
  227.2 2.8 collective-permute-start
  230.0 8.5 %fusion.37 = f32[32,256,128]{2,1,0:T(8,128)} fusion(f32[32,256,128]{2,1,0:T(8,128)} %fusion.4, f32[256,32,128]{2,0,1:T(8,128)} %copy-done.2, f32[256,32,128]{2,0,1:T(8,128)} %copy-done, f32[256,128]{1,0:T(8,128)S(1)} %get-tuple-element.12, f32[256,128]{1,0:T(8,128)S(1)} %get-tuple-element.13), kind=kOutput, calls=%fused_computation.40 | convolution fusion | flops 1616084992 | bytes 17039360 | tf_op jit(solution)/shard_map/ckn,nj->ckj/dot_general | solution.py:58
  238.5 0.3 copy.25
  238.8 0.3 copy.26
  239.1 9.3 %fusion.3 = f32[3,512,1024]{2,1,0:T(8,128)S(1)} fusion(f32[3,512,1023]{2,1,0:T(8,128)} %bitcast.188, f32[3,512,1]{2,1,0:T(8,128)S(1)} %copy.25, f32[3,512,1022]{2,1,0:T(8,128)} %bitcast.189, f32[3,512,2]{2,1,0:T(8,128)S(1)} %copy.26, f32[3,512,1024]{2,1,0:T(8,128)} %copy-done.4, f32[3,512]{1,0:T(4,128)S(1)} %get-tuple-element.10, ...), kind=kLoop, calls=%fused_computation.5 | loop fusion | flops 11010048 | bytes 25184256 | tf_op jit(solution)/shard_map/add | solution.py:103
  248.4 2.7 copy-done.5
  251.1 1.3 fusion.42
  252.4 4.5 all-to-all-start
  256.9 6.8 %fusion.6 = f32[32,256,128]{2,1,0:T(8,128)S(1)} fusion(f32[256,32,128]{2,0,1:T(8,128)} %copy-done.2, f32[256,32,128]{2,0,1:T(8,128)} %copy-done, f32[256,128]{1,0:T(8,128)S(1)} %get-tuple-element.12, f32[256,128]{1,0:T(8,128)S(1)} %get-tuple-element.13), kind=kOutput, calls=%fused_computation.9 | convolution fusion | flops 1615036416 | bytes 12845056 | tf_op jit(solution)/shard_map/ckn,nj->ckj/dot_general | solution.py:55
  263.8 5.7 %fusion.34 = f32[32,256,128]{2,1,0:T(8,128)} fusion(f32[32,256,128]{2,1,0:T(8,128)S(1)} %fusion.6, f32[256,32,128]{2,0,1:T(8,128)S(1)} %copy-done.3, f32[256,32,128]{2,0,1:T(8,128)S(1)} %copy-done.1, f32[256,128]{1,0:T(8,128)S(1)} %get-tuple-element.12, f32[256,128]{1,0:T(8,128)S(1)} %get-tuple-element.13), kind=kOutput, calls=%fused_computation.39 | convolution fusion | flops 1616084992 | bytes 17039360 | tf_op jit(solution)/shard_map/ckn,nj->ckj/dot_general | solution.py:55
  269.5 3.3 all-to-all-done
  272.8 0.6 copy.27
  273.3 1.0 reshape.66
  274.3 2.3 fusion.62
  276.6 2.3 fusion.66
  278.9 4.3 fusion.14
  283.3 5.5 %fusion.12 = f32[32,256,128]{2,1,0:T(8,128)S(1)} fusion(f32[256,32,128]{2,0,1:T(8,128)S(1)} %fusion.66, f32[256,32,128]{2,0,1:T(8,128)S(1)} %fusion.62, f32[256,128]{1,0:T(8,128)} %copy-done.6, f32[256,128]{1,0:T(8,128)} %copy-done.9), kind=kOutput, calls=%fused_computation.15 | convolution fusion | flops 1615036416 | bytes 12845056 | tf_op jit(solution)/shard_map/ckn,nj->ckj/dot_general | solution.py:58
  288.8 5.7 %fusion.28 = f32[32,256,128]{2,1,0:T(8,128)} fusion(f32[32,256,128]{2,1,0:T(8,128)S(1)} %fusion.14, f32[256,32,128]{2,0,1:T(8,128)S(1)} %fusion.66, f32[256,32,128]{2,0,1:T(8,128)S(1)} %fusion.62, f32[256,128]{1,0:T(8,128)S(1)} %copy-done.7, f32[256,128]{1,0:T(8,128)S(1)} %copy-done.10), kind=kOutput, calls=%fused_computation.37 | convolution fusion | flops 1616084992 | bytes 17039360 | tf_op jit(solution)/shard_map/ckn,nj->ckj/dot_general | solution.py:55
  294.6 8.4 %multiply_add_fusion = (f32[32,256,128]{2,1,0:T(8,128)S(1)}, f32[32,256,128]{2,1,0:T(8,128)S(1)}) fusion(f32[32,256,128]{2,1,0:T(8,128)} %fusion.34, f32[32,256,128]{2,1,0:T(8,128)} %fusion.28, f32[32,256,128]{2,1,0:T(8,128)} %fusion.37, f32[32,256,128]{2,1,0:T(8,128)S(1)} %fusion.12, f32[256,128]{1,0:T(8,128)} %copy-done.6, ...), kind=kOutput, calls=%fused_computation.31 | convolution fusion | flops 1622376448 | bytes 33816576 | tf_op jit(solution)/shard_map/ckn,nj->ckj/dot_general | solution.py:58
  303.0 3.8 fusion.100
  306.8 3.7 fusion.102
  310.4 3.8 convolution_add_fusion
  314.3 3.9 convolution_subtract_fusion
  318.2 3.3 fusion.20
  321.5 3.4 multiply_convert_fusion
  324.9 0.7 copy.50
  325.6 0.6 fusion.93
  326.2 0.6 fusion.92
  326.9 0.6 fusion.91
  327.5 0.6 fusion.90
  328.1 0.6 fusion.89
  328.7 0.6 fusion.88
  329.4 0.6 fusion.87
  330.0 0.6 fusion.86
  330.6 0.6 fusion.85
  331.2 0.6 fusion.84
  331.8 0.6 fusion.83
  332.5 0.6 fusion.82
  333.1 0.6 fusion.81
  333.7 0.6 fusion.80
  334.3 0.6 fusion.79
  335.0 0.6 fusion.78
  335.6 4.3 all-to-all-start.2
  340.2 15.6 %all-to-all-done.2 = bf16[16,32,1024]{2,1,0:T(8,128)(2,1)S(1)} async-done(((bf16[16,32,1024]{2,1,0:T(8,128)(2,1)}), bf16[16,32,1024]{2,1,0:T(8,128)(2,1)S(1)}, u32[]{:S(2)}, u32[]{:S(2)}) %all-to-all-start.2) | async-done | bytes 1048608 | tf_op jit(solution)/shard_map/all_to_all | solution.py:9
  355.8 11.3 %convert_bitcast_fusion = bf16[4096,1024]{0,1:T(8,128)(2,1)} fusion(bf16[512,4096]{1,0:T(8,128)(2,1)} %all-gather.8.cloned.1.call-done, f32[3,512,1024]{2,1,0:T(8,128)} %copy-done.5, bf16[512,1024]{1,0:T(8,128)(2,1)S(1)} %bitcast.209, bf16[1,512,1024]{2,1,0:T(8,128)(2,1)} %fusion.42, f32[512]{0:T(512)S(1)} %copy-done.14), kind=kOutput, calls=%fused_computation.2 | convolution fusion | flops 4302307328 | bytes 16779264 | tf_op jit(solution)/shard_map/cd,ct->dt/dot_general | solution.py:123
  367.1 114.3 %reduce-scatter.2.cloned.1.call-done = bf16[512,1024]{0,1:T(8,128)(2,1)} async-done(((bf16[4096,1024]{0,1:T(8,128)(2,1)}), bf16[512,1024]{0,1:T(8,128)(2,1)}) %reduce-scatter.2.cloned.1.call-update) | async-done | bytes 1048592 | tf_op jit(solution)/shard_map/reduce_scatter | solution.py:122
  481.4 2.3 copy.33
  (41 shorter events, 1.0 us)
Async XLA Ops:
  6.5 3.1 copy-start.12
  6.5 120.9 %all-gather.6.cloned.1.call-start = ((), (), s32[]{:S(2)}) async-start(), calls=%async_computation.5 | async-start | bytes 9437184 | tf_op jit(solution)/shard_map/all_gather | solution.py:89
  7.3 12.1 %copy-start.13 = (f32[3,512,3]{1,2,0:T(4,128)S(1)}, f32[3,512,3]{1,2,0:T(4,128)}, u32[]{:S(2)}) copy-start(f32[3,512,3]{1,2,0:T(4,128)} %param.8) | copy-start | bytes 55300
  7.3 200.1 %all-gather.4.cloned.1.call-start = ((), (), s32[]{:S(2)}) async-start(), calls=%async_computation.4 | async-start | bytes 13369344 | tf_op jit(solution)/shard_map/all_gather | solution.py:91
  10.8 28.9 %all-to-all-start.1 = ((bf16[16,32,1024]{2,1,0:T(8,128)(2,1)}), bf16[16,32,1024]{2,1,0:T(8,128)(2,1)S(1)}, u32[]{:S(2)}, u32[]{:S(2)}) async-start(bf16[16,32,1024]{2,1,0:T(8,128)(2,1)} %bitcast.11), calls=%async_computation.1 | async-start | bytes 2097152 | tf_op jit(solution)/shard_map/all_to_all | solution.py:86
  18.6 321.6 %all-gather.8.cloned.1.call-start = ((), (), s32[]{:S(2)}) async-start(), calls=%async_computation.6 | async-start | bytes 4456448 | tf_op jit(solution)/shard_map/all_gather | solution.py:121
  20.0 258.9 %copy-start.6 = (f32[256,128]{1,0:T(8,128)}, f32[256,128]{1,0:T(8,128)S(1)}, u32[]{:S(2)}) copy-start(f32[256,128]{1,0:T(8,128)S(1)} %get-tuple-element.12) | copy-start | bytes 393220
  20.0 258.9 %copy-start.9 = (f32[256,128]{1,0:T(8,128)}, f32[256,128]{1,0:T(8,128)S(1)}, u32[]{:S(2)}) copy-start(f32[256,128]{1,0:T(8,128)S(1)} %get-tuple-element.13) | copy-start | bytes 393220
  43.1 2.4 copy-start
  45.4 2.0 copy-start.2
  224.1 2.6 copy-start.4
  227.2 11.3 %collective-permute-start = (f32[3,512,2]{1,2,0:T(2,128)S(1)}, f32[3,512,2]{1,2,0:T(2,128)S(1)}, u32[]{:S(2)}, u32[]{:S(2)}) collective-permute-start(f32[3,512,2]{1,2,0:T(2,128)S(1)} %copy.24), channel_id=1, source_target_pairs={{0,8},{8,16},{16,24},{24,32},{32,40},{40,48},{48,56},{56,64},{64,7... | collective-permute-start | bytes 36872 | tf_op jit(solution)/shard_map/ppermute | solution.py:22
  248.4 2.7 copy-start.5
  252.4 20.4 %all-to-all-start = ((bf16[16,32,1024]{2,1,0:T(8,128)(2,1)}), bf16[16,32,1024]{2,1,0:T(8,128)(2,1)S(1)}, u32[]{:S(2)}, u32[]{:S(2)}) async-start(bf16[16,32,1024]{2,1,0:T(8,128)(2,1)} %bitcast.3), calls=%async_computation | async-start | bytes 2097152 | tf_op jit(solution)/shard_map/all_to_all | solution.py:108
  256.9 6.8 %copy-start.1 = (f32[256,32,128]{2,0,1:T(8,128)S(1)}, f32[256,32,128]{2,0,1:T(8,128)}, u32[]{:S(2)}) copy-start(f32[256,32,128]{2,0,1:T(8,128)} %copy-done) | copy-start | bytes 12582916
  256.9 6.8 %copy-start.3 = (f32[256,32,128]{2,0,1:T(8,128)S(1)}, f32[256,32,128]{2,0,1:T(8,128)}, u32[]{:S(2)}) copy-start(f32[256,32,128]{2,0,1:T(8,128)} %copy-done.2) | copy-start | bytes 12582916
  283.3 5.5 %copy-start.7 = (f32[256,128]{1,0:T(8,128)S(1)}, f32[256,128]{1,0:T(8,128)}, u32[]{:S(2)}) copy-start(f32[256,128]{1,0:T(8,128)} %copy-done.6) | copy-start | bytes 393220
  283.3 5.5 %copy-start.10 = (f32[256,128]{1,0:T(8,128)S(1)}, f32[256,128]{1,0:T(8,128)}, u32[]{:S(2)}) copy-start(f32[256,128]{1,0:T(8,128)} %copy-done.9) | copy-start | bytes 393220
  314.3 3.9 copy-start.8
  314.3 3.9 copy-start.11
  324.9 30.9 %copy-start.14 = (f32[512]{0:T(512)S(1)}, f32[512]{0:T(512)}, u32[]{:S(2)}) copy-start(f32[512]{0:T(512)} %param.10) | copy-start | bytes 6148
  335.6 20.2 %all-to-all-start.2 = ((bf16[16,32,1024]{2,1,0:T(8,128)(2,1)}), bf16[16,32,1024]{2,1,0:T(8,128)(2,1)S(1)}, u32[]{:S(2)}, u32[]{:S(2)}) async-start(bf16[16,32,1024]{2,1,0:T(8,128)(2,1)} %fusion.78), calls=%async_computation.2 | async-start | bytes 2097152 | tf_op jit(solution)/shard_map/all_to_all | solution.py:9
  339.9 141.5 %reduce-scatter.2.cloned.1.call-start = ((), (), s32[]{:S(2)}) async-start(), calls=%async_computation.7 | async-start | bytes 9437184 | tf_op jit(solution)/shard_map/reduce_scatter | solution.py:122
Sparse Core Ops, SparseCore 0:
  9.7 117.7 all-gather.5
  129.1 78.2 all-gather.3
  209.0 45.4 all-gather.7
  367.2 114.1 reduce-scatter.1
